TPU v7x, 32 devices: a whole 2x2x4 slice. The times are simulated.
32 devices in a mesh: dp: 8 (over z, y), fsdp: 4 (over x, core).
Axes of the slice: x: 2, y: 2, z: 4, core: 2. Of those that a mesh axis runs over, the one named last changes fastest.
Arguments:
- tokens: bfloat16 [16384, 1024], P(('dp', 'fsdp')), may hold values from -6 to 6
- lengths: int32 [32, 4], P(('dp', 'fsdp')), may hold values from 0 to 512, as said below
- w_qkv: bfloat16 [1024, 3072], P(('dp', 'fsdp')), may hold values from -0.1875 to 0.1875
- w_out: bfloat16 [1024, 1024], P(('dp', 'fsdp')), may hold values from -0.75 to 0.75
- w_up: bfloat16 [1024, 4096], P(('dp', 'fsdp')), may hold values from -0.1875 to 0.1875
- w_down: bfloat16 [4096, 1024], P(('dp', 'fsdp')), may hold values from -0.09375 to 0.09375
- gain_attn: bfloat16 [1024], P(('dp', 'fsdp')), may hold values from 0.099609375 to 1.8984375
- gain_mlp: bfloat16 [1024], P(('dp', 'fsdp')), may hold values from 0.099609375 to 1.8984375
- cotangent: bfloat16 [16384, 1024], P(('dp', 'fsdp')), may hold values from -6 to 6
Outputs:
- output: bfloat16 [16384, 1024], P(('dp', 'fsdp'))
- grad_tokens: bfloat16 [16384, 1024], P(('dp', 'fsdp'))
- grad_w_qkv: float32 [1024, 3072], P(('dp', 'fsdp'))
- grad_w_out: float32 [1024, 1024], P(('dp', 'fsdp'))
- grad_w_up: float32 [1024, 4096], P(('dp', 'fsdp'))
- grad_w_down: float32 [4096, 1024], P(('dp', 'fsdp'))
- grad_gain_attn: float32 [1024], P(('dp', 'fsdp'))
- grad_gain_mlp: float32 [1024], P(('dp', 'fsdp'))
Inputs may be any that keep to these rules, and one draw needn't show every extreme that they name: Row b gives the lengths of the items of bucket b in order; empty slots hold 0 and follow the used ones; each row sums to 512; in every draw some bucket holds a single item of 512 frames.
All inputs are finite; a program needn't handle non-finite values.
Results may differ from a plain program's by a relative error of at most 0.012.
Values may be sent and summed in bfloat16 or wider, within the bound.
A program may use at most 192 MiB of HBM per device.

v0:
```python
import math

import jax
import jax.numpy as jnp
from jax import lax
from jax.sharding import PartitionSpec as P

H = 16
HD = 64


epsilon = 1e-05


def normalize(values, gain):
    scale_row = lax.rsqrt(jnp.mean(values * values, axis=-1, keepdims=True) + epsilon)
    return (values * scale_row * gain, scale_row)


def norm_back(grad_normed, values, scale_row, gain):
    scaled = grad_normed * gain
    grad_gain = jnp.sum(grad_normed * values * scale_row, axis=0)
    cubed = scale_row * scale_row * scale_row
    grad_values = scale_row * scaled - values * cubed * jnp.mean(
        scaled * values, axis=-1, keepdims=True
    )
    return (grad_values, grad_gain)


def block_logits(query_block, key_rows, segment):
    block_rows = query_block.shape[0]
    key_limit = key_rows.shape[0]
    raw = jnp.einsum("qhd,khd->hqk", query_block, key_rows, preferred_element_type=jnp.float32)
    query_place = jnp.arange(block_rows, dtype=jnp.int32)
    key_place = jnp.arange(key_limit, dtype=jnp.int32)
    allowed = (segment[:, None] == segment[None, :]) & (query_place[:, None] >= key_place[None, :])
    return jnp.where(allowed[None], raw * (1.0 / math.sqrt(HD)), -1e30)


def attend_forward(queries, keys_all, values_all, segment):
    logits = block_logits(queries, keys_all, segment)
    peak = jnp.max(logits, axis=-1, keepdims=True)
    raised = jnp.exp(logits - peak)
    totals = jnp.sum(raised, axis=-1, keepdims=True)
    attn_prob = (raised / totals).astype(jnp.bfloat16)
    contexts = jnp.einsum("hqk,khd->qhd", attn_prob, values_all, preferred_element_type=jnp.float32)
    log_sums = (peak + jnp.log(totals))[:, :, 0]
    return (contexts, log_sums)


def attend_backward(queries, keys_all, values_all, segment, log_sums, grad_context):
    total_rows = queries.shape[0]
    block_rows = min(512, total_rows)
    grad_keys = jnp.zeros(keys_all.shape, jnp.float32)
    grad_values = jnp.zeros(values_all.shape, jnp.float32)
    logits = block_logits(queries, keys_all, segment)
    attn_prob = jnp.exp(logits - log_sums[:, 0:block_rows, None])
    rounded = attn_prob.astype(jnp.bfloat16)
    grad_prob = jnp.einsum(
        "qhd,khd->hqk", grad_context, values_all, preferred_element_type=jnp.float32
    )
    inner = jnp.sum(attn_prob * grad_prob, axis=-1, keepdims=True)
    grad_logit = (1.0 / math.sqrt(HD) * attn_prob * (grad_prob - inner)).astype(jnp.bfloat16)
    grad_queries = jnp.einsum(
        "hqk,khd->qhd", grad_logit, keys_all, preferred_element_type=jnp.float32
    )
    grad_keys = grad_keys.at[:block_rows].add(
        jnp.einsum("hqk,qhd->khd", grad_logit, queries, preferred_element_type=jnp.float32)
    )
    grad_values = grad_values.at[:block_rows].add(
        jnp.einsum("hqk,qhd->khd", rounded, grad_context, preferred_element_type=jnp.float32)
    )
    return (grad_queries, grad_keys, grad_values)


def gather_forward(w_qkv, w_out, w_up, w_down, gain_attn, gain_mlp):
    return (
        lax.all_gather(w_qkv, ("dp", "fsdp"), axis=0, tiled=True),
        lax.all_gather(w_out, ("dp", "fsdp"), axis=0, tiled=True),
        lax.all_gather(w_up, ("dp", "fsdp"), axis=0, tiled=True),
        lax.all_gather(w_down, ("dp", "fsdp"), axis=0, tiled=True),
        lax.all_gather(gain_attn, ("dp", "fsdp"), axis=0, tiled=True),
        lax.all_gather(gain_mlp, ("dp", "fsdp"), axis=0, tiled=True),
    )


def gather_backward(w_qkv, w_out, w_up, w_down, gain_attn, gain_mlp):
    return (
        lax.all_gather(w_qkv, ("dp", "fsdp"), axis=0, tiled=True),
        lax.all_gather(w_out, ("dp", "fsdp"), axis=0, tiled=True),
        lax.all_gather(w_up, ("dp", "fsdp"), axis=0, tiled=True),
        lax.all_gather(w_down, ("dp", "fsdp"), axis=0, tiled=True),
        lax.all_gather(gain_attn, ("dp", "fsdp"), axis=0, tiled=True),
        lax.all_gather(gain_mlp, ("dp", "fsdp"), axis=0, tiled=True),
    )


def sum_gradients(grad_qkv, grad_out, grad_up, grad_down, grad_gain_a, grad_gain_m):
    return (
        lax.psum_scatter(grad_qkv, ("dp", "fsdp"), scatter_dimension=0, tiled=True),
        lax.psum_scatter(grad_out, ("dp", "fsdp"), scatter_dimension=0, tiled=True),
        lax.psum_scatter(grad_up, ("dp", "fsdp"), scatter_dimension=0, tiled=True),
        lax.psum_scatter(grad_down, ("dp", "fsdp"), scatter_dimension=0, tiled=True),
        lax.psum_scatter(grad_gain_a, ("dp", "fsdp"), scatter_dimension=0, tiled=True),
        lax.psum_scatter(grad_gain_m, ("dp", "fsdp"), scatter_dimension=0, tiled=True),
    )


def project_input(inputs, weights):
    normed, scale_one = normalize(inputs, weights[4].astype(jnp.float32))
    normed_low = normed.astype(jnp.bfloat16)
    mixed = jnp.dot(normed_low, weights[0], preferred_element_type=jnp.float32).astype(jnp.bfloat16)
    split = mixed.reshape(inputs.shape[0], 3, H, HD)
    return (normed_low, scale_one, split[:, 0], split[:, 1], split[:, 2])


def feed_inputs(inputs, context, weights):
    middle = inputs + jnp.dot(context, weights[1], preferred_element_type=jnp.float32)
    second, scale_two = normalize(middle, weights[5].astype(jnp.float32))
    second_low = second.astype(jnp.bfloat16)
    hidden = jnp.dot(second_low, weights[2], preferred_element_type=jnp.float32)
    active = jax.nn.gelu(hidden, approximate=True).astype(jnp.bfloat16)
    return (middle, scale_two, second_low, hidden, active)


def shards(tokens, lengths, w_qkv, w_out, w_up, w_down, gain_attn, gain_mlp, cotangent):
    total_rows = tokens.shape[0]
    ends = jnp.cumsum(lengths[0])
    places = jnp.arange(total_rows, dtype=jnp.int32)
    segment = jnp.sum((places[:, None] >= ends[None, :]).astype(jnp.int32), axis=1)
    inputs = tokens.astype(jnp.float32)
    weights = gather_forward(w_qkv, w_out, w_up, w_down, gain_attn, gain_mlp)
    normed_low, scale_one, queries, keys_all, values_all = project_input(inputs, weights)
    context_full, log_sums = attend_forward(queries, keys_all, values_all, segment)
    context = context_full.reshape(total_rows, H * HD).astype(jnp.bfloat16)
    middle, scale_two, second_low, hidden, active = feed_inputs(inputs, context, weights)
    output = (middle + jnp.dot(active, weights[3], preferred_element_type=jnp.float32)).astype(
        jnp.bfloat16
    )
    weights = gather_backward(w_qkv, w_out, w_up, w_down, gain_attn, gain_mlp)
    normed_low, scale_one, queries, keys_all, values_all = project_input(inputs, weights)
    middle, scale_two, second_low, hidden, active = feed_inputs(inputs, context, weights)
    grad_down = jnp.einsum("rf,rd->fd", active, cotangent, preferred_element_type=jnp.float32)
    grad_active = jnp.einsum("rd,fd->rf", cotangent, weights[3], preferred_element_type=jnp.float32)
    unused, gelu_pull = jax.vjp(lambda values: jax.nn.gelu(values, approximate=True), hidden)
    grad_hidden = gelu_pull(grad_active)[0].astype(jnp.bfloat16)
    grad_up = jnp.einsum("rd,rf->df", second_low, grad_hidden, preferred_element_type=jnp.float32)
    grad_second = jnp.einsum(
        "rf,df->rd", grad_hidden, weights[2], preferred_element_type=jnp.float32
    )
    grad_mid_norm, grad_gain_m = norm_back(
        grad_second, middle, scale_two, weights[5].astype(jnp.float32)
    )
    grad_middle = cotangent.astype(jnp.float32) + grad_mid_norm
    grad_mid_low = grad_middle.astype(jnp.bfloat16)
    grad_out = jnp.einsum("rc,rd->cd", context, grad_mid_low, preferred_element_type=jnp.float32)
    grad_context = jnp.einsum(
        "rd,cd->rc", grad_mid_low, weights[1], preferred_element_type=jnp.float32
    )
    grad_context = grad_context.astype(jnp.bfloat16).reshape(total_rows, H, HD)
    grad_queries, grad_keys, grad_values = attend_backward(
        queries, keys_all, values_all, segment, log_sums, grad_context
    )
    grad_mixed = (
        jnp.stack([grad_queries, grad_keys, grad_values], axis=1)
        .reshape(total_rows, 3 * H * HD)
        .astype(jnp.bfloat16)
    )
    grad_qkv = jnp.einsum("rd,re->de", normed_low, grad_mixed, preferred_element_type=jnp.float32)
    grad_normed = jnp.einsum(
        "re,de->rd", grad_mixed, weights[0], preferred_element_type=jnp.float32
    )
    grad_in_norm, grad_gain_a = norm_back(
        grad_normed, inputs, scale_one, weights[4].astype(jnp.float32)
    )
    grad_tokens = (grad_middle + grad_in_norm).astype(jnp.bfloat16)
    summed = sum_gradients(grad_qkv, grad_out, grad_up, grad_down, grad_gain_a, grad_gain_m)
    return (output, grad_tokens, summed[0], summed[1], summed[2], summed[3], summed[4], summed[5])


def solution(mesh):
    placed = (
        P(("dp", "fsdp"), None),
        P(("dp", "fsdp"), None),
        P(("dp", "fsdp"), None),
        P(("dp", "fsdp"), None),
        P(("dp", "fsdp"), None),
        P(("dp", "fsdp"), None),
        P(("dp", "fsdp")),
        P(("dp", "fsdp")),
        P(("dp", "fsdp"), None),
    )
    return jax.shard_map(
        shards,
        mesh=mesh,
        in_specs=placed,
        out_specs=(
            P(("dp", "fsdp"), None),
            P(("dp", "fsdp"), None),
            P(("dp", "fsdp"), None),
            P(("dp", "fsdp"), None),
            P(("dp", "fsdp"), None),
            P(("dp", "fsdp"), None),
            P(("dp", "fsdp")),
            P(("dp", "fsdp")),
        ),
        check_vma=False,
    )
```

profile of v0, /device:TPU:0, one launch (start us, length us, event | category | flops | bytes accessed | tf_op | source)
XLA Modules:
  0.0 1005.6 jit_solution(17011372090039116390)
XLA Ops:
  7.2 0.7 all-gather.5.cloned.1.call-update
  7.9 0.7 all-gather.7.cloned.1.call-update
  8.7 0.7 all-gather.11.cloned.1.call-update
  10.0 0.8 dynamic-update-slice.4
  10.9 0.8 dynamic-update-slice.5
  11.7 42.3 %all-reduce.5 = (bf16[1024]{0:T(1024)(128)(2,1)S(1)}, bf16[1024]{0:T(1024)(128)(2,1)S(1)}) all-reduce(bf16[1024]{0:T(1024)(128)(2,1)S(1)} %dynamic-update-slice.4, bf16[1024]{0:T(1024)(128)(2,1)S(1)} %dynamic-update-slice.5), channel_id=1, replica_groups=mesh['dp'=8,'fsdp'=4] {'dp','fsdp'}, use_global_device_ids=true, to_apply=%add | all-reduce | flops 2048 | bytes 8192
  54.1 0.8 reduce-window.8
  55.0 1.5 fusion.13
  56.5 0.6 multiply_multiply_fusion.2
  57.3 26.0 %all-gather.5.cloned.1.call-done = bf16[1024,3072]{1,0:T(8,128)(2,1)} async-done(((bf16[32,3072]{1,0:T(8,128)(2,1)}), bf16[1024,3072]{1,0:T(8,128)(2,1)}) %all-gather.5.cloned.1.call-update) | async-done | bytes 6291472 | tf_op jit(solution)/shard_map/all_gather | solution.py:78
  83.2 8.3 convolution_convert_fusion
  91.5 3.2 copy.38
  94.7 7.3 fusion.43
  102.0 8.3 fusion
  110.3 8.9 fusion.23
  119.2 21.8 %all-gather.7.cloned.1.call-done = bf16[1024,1024]{1,0:T(8,128)(2,1)} async-done(((bf16[32,1024]{1,0:T(8,128)(2,1)}), bf16[1024,1024]{1,0:T(8,128)(2,1)}) %all-gather.7.cloned.1.call-update) | async-done | bytes 2097168 | tf_op jit(solution)/shard_map/all_gather | solution.py:79
  141.0 4.8 multiply_reduce_fusion.3
  145.8 74.4 %all-gather.11.cloned.1.call-done = bf16[4096,1024]{1,0:T(8,128)(2,1)} async-done(((bf16[128,1024]{1,0:T(8,128)(2,1)}), bf16[4096,1024]{1,0:T(8,128)(2,1)}) %all-gather.11.cloned.1.call-update) | async-done | bytes 8388624 | tf_op jit(solution)/shard_map/all_gather | solution.py:81
  220.2 11.5 %fusion.44 = f32[512,4096]{1,0:T(8,128)} fusion(bf16[512,1024]{1,0:T(8,128)(2,1)} %param.25, bf16[4096,1024]{1,0:T(8,128)(2,1)} %all-gather.11.cloned.1.call-done), kind=kOutput, calls=%fused_computation.76 | convolution fusion | flops 4294967296 | bytes 17825792 | tf_op jit(solution)/shard_map/rd,fd->rf/dot_general | solution.py:144
  231.7 67.3 %all-gather.9.cloned.1.call-done = bf16[1024,4096]{1,0:T(8,128)(2,1)} async-done(((bf16[32,4096]{1,0:T(8,128)(2,1)}), bf16[1024,4096]{1,0:T(8,128)(2,1)}) %all-gather.9.cloned.1.call-update) | async-done | bytes 8388624 | tf_op jit(solution)/shard_map/all_gather | solution.py:80
  299.0 16.3 %fusion.8 = (bf16[512,4096]{1,0:T(8,128)(2,1)}, f32[512,4096]{1,0:T(8,128)}) fusion(f32[512,4096]{1,0:T(8,128)} %fusion.44, bf16[1024,4096]{1,0:T(8,128)(2,1)} %all-gather.9.cloned.1.call-done, f32[512,1024]{1,0:T(8,128)} %get-tuple-element.63, f32[1024]{0:T(1024)S(1)} %convert_element_type.81, f32[512]{0:T(512)S(1)} %get-tuple-element.59), kind=kOutput, calls=%fused_computation.16 | convolution fusion | flops 4338483200 | bytes 31463424 | tf_op jit(solution)/shard_map/dot_general | solution.py:121
  315.3 7.7 multiply_reduce_fusion.1
  323.1 0.6 subtract_add_fusion
  323.7 1.3 copy-done.1
  325.0 3.3 fusion.34
  328.4 4.5 convolution_convert_fusion.3
  332.9 2.3 copy.40
  335.2 11.2 %multiply_reduce_fusion = (f32[16,512]{1,0:T(8,128)S(1)}, f32[16,512,512]{1,2,0:T(8,128)}) fusion(f32[16,512,512]{1,2,0:T(8,128)} %get-tuple-element.61, f32[16,512]{1,0:T(8,128)S(1)} %log_add_fusion, bf16[512,16,64]{0,2,1:T(8,128)(2,1)} %bitcast.65, bf16[512,3,16,64]{0,3,2,1:T(8,128)(2,1)S(1)} %bitcast.62), kind=kOutput, calls=%fused_computation.1 | convolution fusion | flops 549445632 | bytes 35717120 | tf_op jit(solution)/shard_map/qhd,khd->hqk/dot_general | solution.py:59
  346.4 16.0 %multiply_convert_fusion = bf16[16,512,512]{1,2,0:T(8,128)(2,1)} fusion(f32[16,512,512]{1,2,0:T(8,128)} %get-tuple-element.68, f32[16,512,512]{1,2,0:T(8,128)} %get-tuple-element.61, f32[16,512]{1,0:T(8,128)S(1)} %get-tuple-element.67, f32[16,512]{1,0:T(8,128)S(1)} %log_add_fusion), kind=kLoop, calls=%fused_computation | loop fusion | flops 20971520 | bytes 42008576 | tf_op jit(solution)/shard_map/convert_element_type | solution.py:63
  362.5 7.4 fusion.31
  369.9 6.3 fusion.30
  376.2 4.4 fusion.27
  380.6 2.3 pad_maximum_fusion
  382.9 1.8 copy-done.9
  384.7 6.7 fusion.37
  391.7 0.9 copy-done.11
  392.7 15.0 %fusion.42 = f32[4096,1024]{1,0:T(8,128)} fusion(bf16[512,1024]{1,0:T(8,128)(2,1)S(1)} %copy-done.11, f32[512,4096]{1,0:T(8,128)} %get-tuple-element.65), kind=kOutput, calls=%fused_computation.74 | convolution fusion | flops 4313841664 | bytes 26214400 | tf_op jit(solution)/shard_map/rf,rd->fd/dot_general | solution.py:143
  407.7 1.5 copy-done.6
  409.3 10.5 %fusion.40 = f32[1024,4096]{1,0:T(8,128)} fusion(bf16[512,4096]{1,0:T(8,128)(2,1)} %get-tuple-element.64, f32[512,1024]{1,0:T(8,128)S(1)} %copy-done.6, f32[1024]{0:T(1024)S(1)} %convert_element_type.81, f32[512]{0:T(512)S(1)} %copy-done.15), kind=kOutput, calls=%fused_computation.72 | convolution fusion | flops 4296540160 | bytes 23074816 | tf_op jit(solution)/shard_map/rd,rf->df/dot_general | solution.py:147
  419.9 8.9 fusion.22
  428.8 40.0 %all-reduce.4 = (f32[1024]{0:T(1024)S(1)}, f32[1024]{0:T(1024)S(1)}) all-reduce(f32[1024]{0:T(1024)S(1)} %get-tuple-element.50, f32[1024]{0:T(1024)S(1)} %copy-done.16), channel_id=6, replica_groups=mesh['dp'=8,'fsdp'=4] {'dp','fsdp'}, use_global_device_ids=true, to_apply=%region_14.15.clone | all-reduce | flops 2048 | bytes 16384
  468.8 0.6 dynamic-slice.10
  469.4 0.6 dynamic-slice.11
  470.0 3.1 fusion.19
  473.1 12.5 %add_convert_fusion = bf16[512,1024]{1,0:T(8,128)(2,1)} fusion(f32[512,1024]{1,0:T(8,128)S(1)} %copy-done.7, bf16[4096,1024]{1,0:T(8,128)(2,1)} %all-gather.11.cloned.1.call-done, f32[512,4096]{1,0:T(8,128)} %get-tuple-element.65), kind=kOutput, calls=%fused_computation.42 | convolution fusion | flops 4314890240 | bytes 19922944 | tf_op jit(solution)/shard_map/dot_general | solution.py:137
  485.6 140.4 %reduce-scatter.5.cloned.1.call-done = f32[32,3072]{1,0:T(8,128)} async-done(((f32[1024,3072]{1,0:T(8,128)}), f32[32,3072]{1,0:T(8,128)}) %reduce-scatter.5.cloned.1.call-update) | async-done | bytes 393232 | tf_op jit(solution)/shard_map/reduce_scatter | solution.py:100
  626.0 184.8 %reduce-scatter.11.cloned.1.call-done = f32[128,1024]{1,0:T(8,128)} async-done(((f32[4096,1024]{1,0:T(8,128)}), f32[128,1024]{1,0:T(8,128)}) %reduce-scatter.11.cloned.1.call-update) | async-done | bytes 524304 | tf_op jit(solution)/shard_map/reduce_scatter | solution.py:103
  810.8 187.4 %reduce-scatter.9.cloned.1.call-done = f32[32,4096]{1,0:T(8,128)} async-done(((f32[1024,4096]{1,0:T(8,128)}), f32[32,4096]{1,0:T(8,128)}) %reduce-scatter.9.cloned.1.call-update) | async-done | bytes 524304 | tf_op jit(solution)/shard_map/reduce_scatter | solution.py:102
  (65 shorter events, 1.5 us)
Async XLA Ops:
  7.2 76.1 %all-gather.5.cloned.1.call-start = ((), (), s32[]{:S(2)}) async-start(), calls=%async_computation.4 | async-start | bytes 6488064 | tf_op jit(solution)/shard_map/all_gather | solution.py:78
  7.9 133.1 %all-gather.7.cloned.1.call-start = ((), (), s32[]{:S(2)}) async-start(), calls=%async_computation.5 | async-start | bytes 2162688 | tf_op jit(solution)/shard_map/all_gather | solution.py:79
  8.6 211.6 %all-gather.11.cloned.1.call-start = ((), (), s32[]{:S(2)}) async-start(), calls=%async_computation.7 | async-start | bytes 8650752 | tf_op jit(solution)/shard_map/all_gather | solution.py:81
  9.4 289.6 %all-gather.9.cloned.1.call-start = ((), (), s32[]{:S(2)}) async-start(), calls=%async_computation.6 | async-start | bytes 8650752 | tf_op jit(solution)/shard_map/all_gather | solution.py:80
  10.0 475.7 %reduce-scatter.7.cloned.1.call-start = ((), (), s32[]{:S(2)}) async-start(), calls=%async_computation.9 | async-start | bytes 4325376 | tf_op jit(solution)/shard_map/reduce_scatter | solution.py:101
  94.7 267.8 %copy-start = (bf16[512,3072]{0,1:T(8,128)(2,1)}, bf16[512,3072]{0,1:T(8,128)(2,1)S(1)}, u32[]{:S(2)}) copy-start(bf16[512,3072]{0,1:T(8,128)(2,1)S(1)} %copy.38) | copy-start | bytes 9437188
  145.8 177.3 %copy-start.14 = (f32[512]{0:T(512)}, f32[512]{0:T(512)S(1)}, u32[]{:S(2)}) copy-start(f32[512]{0:T(512)S(1)} %get-tuple-element.59) | copy-start | bytes 6148
  299.0 16.3 %copy-start.5 = (f32[512,1024]{1,0:T(8,128)S(1)}, f32[512,1024]{1,0:T(8,128)}, u32[]{:S(2)}) copy-start(f32[512,1024]{1,0:T(8,128)} %get-tuple-element.63) | copy-start | bytes 6291460
  299.0 16.3 %copy-start.17 = (bf16[1024,4096]{1,0:T(8,128)(2,1)S(1)}, bf16[1024,4096]{1,0:T(8,128)(2,1)}, u32[]{:S(2)}) copy-start(bf16[1024,4096]{1,0:T(8,128)(2,1)} %all-gather.9.cloned.1.call-done) | copy-start | bytes 25165828
  315.3 7.7 copy-start.10
  323.1 1.9 copy-start.8
  323.7 1.3 copy-start.1
  328.3 297.7 %reduce-scatter.5.cloned.1.call-start = ((), (), s32[]{:S(2)}) async-start(), calls=%async_computation.8 | async-start | bytes 12976128 | tf_op jit(solution)/shard_map/reduce_scatter | solution.py:100
  328.4 18.0 %copy-start.12 = (f32[16,512]{1,0:T(8,128)}, f32[16,512]{1,0:T(8,128)S(1)}, u32[]{:S(2)}) copy-start(f32[16,512]{1,0:T(8,128)S(1)} %log_add_fusion) | copy-start | bytes 98308
  346.4 29.8 %slice-start = ((s8[16777216]{0:T(1024)(128)(4,1)}), s8[4194304]{0:T(1024)(128)(4,1)S(1)}, s32[]{:S(2)}) async-start(s8[16777216]{0:T(1024)(128)(4,1)} %bitcast.58), calls=%async_computation.12 | async-start | bytes 8388608
  346.4 29.8 %slice-start.1 = ((s8[16777216]{0:T(1024)(128)(4,1)}), s8[4194304]{0:T(1024)(128)(4,1)S(1)}, s32[]{:S(2)}) async-start(s8[16777216]{0:T(1024)(128)(4,1)} %bitcast.58), calls=%async_computation.13 | async-start | bytes 8388608
  346.4 29.8 %slice-start.2 = ((s8[16777216]{0:T(1024)(128)(4,1)}), s8[4194304]{0:T(1024)(128)(4,1)S(1)}, s32[]{:S(2)}) async-start(s8[16777216]{0:T(1024)(128)(4,1)} %bitcast.58), calls=%async_computation.14 | async-start | bytes 8388608
  369.9 6.3 slice-start.3
  369.9 6.3 copy-start.3
  380.6 4.1 copy-start.4
  382.9 1.8 copy-start.9
  391.4 1.2 copy-start.11
  391.5 419.4 %reduce-scatter.11.cloned.1.call-start = ((), (), s32[]{:S(2)}) async-start(), calls=%async_computation.11 | async-start | bytes 17301504 | tf_op jit(solution)/shard_map/reduce_scatter | solution.py:103
  407.7 1.6 copy-start.6
  407.7 1.6 copy-start.15
  407.7 590.6 %reduce-scatter.9.cloned.1.call-start = ((), (), s32[]{:S(2)}) async-start(), calls=%async_computation.10 | async-start | bytes 17301504 | tf_op jit(solution)/shard_map/reduce_scatter | solution.py:102
  419.8 9.0 copy-start.16
  419.8 50.1 %copy-start.2 = (f32[512,1024]{1,0:T(8,128)S(1)}, f32[512,1024]{1,0:T(8,128)}, u32[]{:S(2)}) copy-start(f32[512,1024]{1,0:T(8,128)} %copy-done.1) | copy-start | bytes 6291460
  419.8 50.1 %copy-start.13 = (f32[512]{0:T(512)S(1)}, f32[512]{0:T(512)}, u32[]{:S(2)}) copy-start(f32[512]{0:T(512)} %get-tuple-element.56) | copy-start | bytes 6148
  468.8 4.3 copy-start.7
Sparse Core Ops, SparseCore 0:
  10.9 72.3 all-gather.4
  86.1 54.8 all-gather.6
  143.9 76.2 all-gather.10
  222.9 76.0 all-gather.8
  328.5 139.7 reduce-scatter.6
  474.7 151.2 reduce-scatter.4
  629.0 181.8 reduce-scatter.10
  813.8 184.4 reduce-scatter.8
where the time goes:
time: 1010 us
  waiting for transfers between devices  705 us (70%)
  matrix products  156 us (15%)
  blocking collectives  82.4 us (8%)
  other arithmetic  33.5 us (3%)
  between operations  14.8 us (1%)
  local copies, waits for them, and re-layouts  14 us (1%)
    reduce_scatter x1, waiting for transfers between devices, sum_gradients(): lax.psum_scatter(grad_up, ('dp', 'fsdp'), scatter_dimension=0, tiled=True)  187 us
    reduce_scatter x1, waiting for transfers between devices, sum_gradients(): lax.psum_scatter(grad_down, ('dp', 'fsdp'), scatter_dimension=0, tiled=True)  185 us
    reduce_scatter x1, waiting for transfers between devices, sum_gradients(): lax.psum_scatter(grad_qkv, ('dp', 'fsdp'), scatter_dimension=0, tiled=True)  140 us
    unnamed x2, blocking collectives  82.4 us
    all_gather x1, waiting for transfers between devices, gather_forward(): lax.all_gather(w_down, ('dp', 'fsdp'), axis=0, tiled=True)  74.4 us
    all_gather x1, waiting for transfers between devices, gather_forward(): lax.all_gather(w_up, ('dp', 'fsdp'), axis=0, tiled=True)  67.3 us
    all_gather x1, waiting for transfers between devices, gather_forward(): lax.all_gather(w_qkv, ('dp', 'fsdp'), axis=0, tiled=True)  26 us
    all_gather x1, waiting for transfers between devices, gather_forward(): lax.all_gather(w_out, ('dp', 'fsdp'), axis=0, tiled=True)  21.8 us
  transfers between devices with their start and end apart: 8, of which 7 were waited for; matrix products, arithmetic and copies ran while one was open for 17% of the time, Pallas kernels for 0%

commit v1 on v0

v1 whole, which is shorter than its diff:
```python
import functools
import math

import jax
import jax.numpy as jnp
from jax import lax
from jax.experimental import pallas as pl
from jax.experimental.pallas import tpu as pltpu
from jax.sharding import PartitionSpec as P

H = 16
HD = 64
MESH = pl.DeviceIdType.MESH
AXES = ("dp", "fsdp")


epsilon = 1e-05


def normalize(values, gain):
    scale_row = lax.rsqrt(jnp.mean(values * values, axis=-1, keepdims=True) + epsilon)
    return (values * scale_row * gain, scale_row)


def norm_back(grad_normed, values, scale_row, gain):
    scaled = grad_normed * gain
    grad_gain = jnp.sum(grad_normed * values * scale_row, axis=0)
    cubed = scale_row * scale_row * scale_row
    grad_values = scale_row * scaled - values * cubed * jnp.mean(
        scaled * values, axis=-1, keepdims=True
    )
    return (grad_values, grad_gain)


def block_logits(query_block, key_rows, segment):
    block_rows = query_block.shape[0]
    key_limit = key_rows.shape[0]
    raw = jnp.einsum("qhd,khd->hqk", query_block, key_rows, preferred_element_type=jnp.float32)
    query_place = jnp.arange(block_rows, dtype=jnp.int32)
    key_place = jnp.arange(key_limit, dtype=jnp.int32)
    allowed = (segment[:, None] == segment[None, :]) & (query_place[:, None] >= key_place[None, :])
    return jnp.where(allowed[None], raw * (1.0 / math.sqrt(HD)), -1e30)


def attend_forward(queries, keys_all, values_all, segment):
    logits = block_logits(queries, keys_all, segment)
    peak = jnp.max(logits, axis=-1, keepdims=True)
    raised = jnp.exp(logits - peak)
    totals = jnp.sum(raised, axis=-1, keepdims=True)
    attn_prob = (raised / totals).astype(jnp.bfloat16)
    contexts = jnp.einsum("hqk,khd->qhd", attn_prob, values_all, preferred_element_type=jnp.float32)
    log_sums = (peak + jnp.log(totals))[:, :, 0]
    return (contexts, log_sums)


def attend_backward(queries, keys_all, values_all, segment, log_sums, grad_context):
    logits = block_logits(queries, keys_all, segment)
    attn_prob = jnp.exp(logits - log_sums[:, :, None])
    rounded = attn_prob.astype(jnp.bfloat16)
    grad_prob = jnp.einsum(
        "qhd,khd->hqk", grad_context, values_all, preferred_element_type=jnp.float32
    )
    inner = jnp.sum(attn_prob * grad_prob, axis=-1, keepdims=True)
    grad_logit = (1.0 / math.sqrt(HD) * attn_prob * (grad_prob - inner)).astype(jnp.bfloat16)
    grad_queries = jnp.einsum(
        "hqk,khd->qhd", grad_logit, keys_all, preferred_element_type=jnp.float32
    )
    grad_keys = jnp.einsum("hqk,qhd->khd", grad_logit, queries, preferred_element_type=jnp.float32)
    grad_values = jnp.einsum(
        "hqk,qhd->khd", rounded, grad_context, preferred_element_type=jnp.float32
    )
    return (grad_queries, grad_keys, grad_values)


def gather_any(*weights):
    return tuple(lax.all_gather(w, AXES, axis=0, tiled=True) for w in weights)


def sum_any(*grads):
    return tuple(lax.psum_scatter(g, AXES, scatter_dimension=0, tiled=True) for g in grads)


NZ = 4


def coords():
    a, b = lax.axis_index("dp"), lax.axis_index("fsdp")
    return a // 2, a % 2, b // 2, b % 2


def device(z, y, x, c):
    return (z * 2 + y, x * 2 + c)


def owner(z, y, x, c):
    return ((z * 2 + y) * 2 + x) * 2 + c


def all_peers(z, y, x, c):
    peers = []
    for d in range(NZ):
        for m in range(2):
            for l in range(2):
                for s in range(2):
                    if d + m + l + s:
                        peers.append(
                            device(
                                lax.rem(z + d, NZ),
                                1 - y if m else y,
                                1 - x if l else x,
                                1 - c if s else c,
                            )
                        )
    return peers


def greet(peers):
    sem = pltpu.get_barrier_semaphore()
    for peer in peers:
        pl.semaphore_signal(sem, inc=1, device_id=peer, device_id_type=MESH)
    pl.semaphore_wait(sem, len(peers))


def remote(src, dst, send_sem, recv_sem, peer):
    return pltpu.make_async_remote_copy(
        src_ref=src, dst_ref=dst, send_sem=send_sem, recv_sem=recv_sem,
        device_id=peer, device_id_type=MESH,
    )


def gather_kernel(nw, *refs):
    ins, outs = refs[:nw], refs[nw : 2 * nw]
    gain_in, gain_out = refs[2 * nw], refs[2 * nw + 1]
    lsem, ssem, rsem, gs, gr = refs[2 * nw + 2 :]
    z, y, x, c = coords()
    zfrom = [lax.rem(z + NZ - d, NZ) for d in range(NZ)]
    ypeer, xpeer, speer = device(z, 1 - y, x, c), device(z, y, 1 - x, c), device(z, y, x, 1 - c)
    zpeers = [device(lax.rem(z + d, NZ), y, x, c) for d in range(1, NZ)]
    peers = all_peers(z, y, x, c)
    greet(peers)
    pend = []
    me = owner(z, y, x, c)
    gain_copies = []
    for j, peer in enumerate(peers):
        cp = remote(gain_in, gain_out.at[j + 1], gs.at[j], gr.at[j], peer)
        cp.start()
        gain_copies.append(cp)
    own_gain = pltpu.make_async_copy(gain_in, gain_out.at[0], lsem.at[nw])
    own_gain.start()

    def rows(w, p, o):
        r = ins[w].shape[0] // 2
        return pl.ds(pl.multiple_of(o * (2 * r) + p * r, r), r)

    def send(w, p, o, k, peer, own=False):
        r = ins[w].shape[0] // 2
        dst = outs[w].at[rows(w, p, o)]
        src = ins[w].at[pl.ds(p * r, r)] if own else dst
        cp = remote(src, dst, ssem.at[w, p, k], rsem.at[w, p, k], peer)
        cp.start()
        pend.append(cp)

    def wait(w, p, o, k):
        ref = outs[w].at[rows(w, p, o)]
        remote(ref, ref, ssem.at[w, p, k], rsem.at[w, p, k], speer).wait_recv()

    def sib(w, p, o, i, own=False):
        send(w, p, o, 15 + i, speer, own)

    def whose(p, d, m, l, core):
        sy, sx = (m, l) if p == 0 else (l, m)
        return owner(zfrom[d], (1 - y) if sy else y, (1 - x) if sx else x, core)

    second, third = [ypeer, xpeer], [xpeer, ypeer]
    local = [own_gain]

    def start(w):
        for p in range(2):
            o = whose(p, 0, 0, 0, c)
            send(w, p, o, 3, second[p], True)
            send(w, p, o, 7, third[p], True)
            for d in range(1, NZ):
                send(w, p, o, d - 1, zpeers[d - 1], True)
            sib(w, p, o, 0, True)
        n = ins[w].shape[0]
        cp = pltpu.make_async_copy(
            ins[w], outs[w].at[pl.ds(pl.multiple_of(me * n, n), n)], lsem.at[w]
        )
        cp.start()
        local.append(cp)

    def from_z(w):
        for d in (1, 3, 2):
            for p in range(2):
                o = whose(p, d, 0, 0, c)
                wait(w, p, o, d - 1)
                send(w, p, o, 3 + d, second[p])
                send(w, p, o, 7 + d, third[p])
                sib(w, p, o, d)

    def from_second(w):
        for d in (0, 1, 3, 2):
            for p in range(2):
                o = whose(p, d, 1, 0, c)
                wait(w, p, o, 3 + d)
                send(w, p, o, 11 + d, third[p])
                sib(w, p, o, 4 + d)

    def from_third(w):
        for m in (0, 1):
            for d in (0, 1, 3, 2):
                for p in range(2):
                    o = whose(p, d, m, 1, c)
                    wait(w, p, o, 7 + m * 4 + d)
                    sib(w, p, o, 8 + m * 4 + d)

    def from_core(w):
        for p in range(2):
            for l in (0, 1):
                for m in (0, 1):
                    for d in range(4):
                        wait(w, p, whose(p, d, m, l, 1 - c), 15 + l * 8 + m * 4 + d)

    for t in range(nw + 4):
        for step, lag in ((start, 0), (from_z, 1), (from_second, 2), (from_third, 3), (from_core, 4)):
            if 0 <= t - lag < nw:
                step(t - lag)
    for cp in gain_copies:
        cp.wait()
    for cp in pend:
        cp.wait_send()
    for cp in local:
        cp.wait()


def gather(weights, gains):
    nw = len(weights)
    hbm = pl.BlockSpec(memory_space=pl.ANY)
    out = pl.pallas_call(
        functools.partial(gather_body, nw),
        out_shape=[jax.ShapeDtypeStruct((w.shape[0] * 32, w.shape[1]), w.dtype) for w in weights]
        + [jax.ShapeDtypeStruct((32, 8, 128), jnp.float32)],
        in_specs=[hbm] * (nw + 1),
        out_specs=[hbm] * (nw + 1),
        scratch_shapes=[
            pltpu.SemaphoreType.DMA((nw + 1,)),
            pltpu.SemaphoreType.DMA((nw, 2, 31)),
            pltpu.SemaphoreType.DMA((nw, 2, 31)),
            pltpu.SemaphoreType.DMA((31,)),
            pltpu.SemaphoreType.DMA((31,)),
        ],
        compiler_params=pltpu.CompilerParams(collective_id=0, has_side_effects=True),
    )(*weights, gains)
    return out[:nw], out[nw]


def gather_body(nw, *refs):
    ins, gain_in = refs[:nw], refs[nw]
    outs, gain_out = refs[nw + 1 : 2 * nw + 1], refs[2 * nw + 1]
    gather_kernel(nw, *ins, *outs, gain_in, gain_out, *refs[2 * nw + 2 :])


UNITS = ((0, 0, 1024), (1, 0, 4096), (2, 0, 1024), (3, 0, 1024), (3, 1024, 1024), (3, 2048, 1024))


def scatter_kernel(dims, *refs):
    nu = len(UNITS)
    grads, gain_in = refs[:4], refs[4]
    outs, gain_out = refs[5:9], refs[9]
    refs = refs[10:]
    mine, got0, got1, got2, got3, res = (refs[i * nu : (i + 1) * nu] for i in range(6))
    got_gain, ssem, rsem, lsem, osem, gs, gr = refs[6 * nu :]
    z, y, x, c = coords()
    ypeer, xpeer, speer = device(z, 1 - y, x, c), device(z, y, 1 - x, c), device(z, y, x, 1 - c)
    zof = [lax.rem(z + d, NZ) for d in range(NZ)]
    zpeers = [device(zof[d], y, x, c) for d in range(NZ)]
    peers = all_peers(z, y, x, c)
    greet(peers)
    pend = []

    def send(u, k, src, dst, peer):
        cp = remote(src, dst, ssem.at[u, k], rsem.at[u, k], peer)
        cp.start()
        pend.append(cp)

    def wait(u, k, ref):
        remote(ref, ref, ssem.at[u, k], rsem.at[u, k], speer).wait_recv()

    def add(dst, src):
        dst[...] = (dst[...].astype(jnp.float32) + src[...].astype(jnp.float32)).astype(dst.dtype)

    def stage0(u):
        w, col, width = UNITS[u]
        src = grads[w].at[:, :, :, :, :, pl.ds(col, width)]
        send(u, 0, src.at[:, :, :, 1 - c], got0[u], speer)
        cp = pltpu.make_async_copy(src.at[:, :, :, c], mine[u], lsem.at[u])
        cp.start()

    def stage1(u):
        w, col, width = UNITS[u]
        src = grads[w].at[:, :, :, c, :, pl.ds(col, width)]
        h = mine[u].shape[3] // 2
        pltpu.make_async_copy(src, mine[u], lsem.at[u]).wait()
        wait(u, 0, got0[u])
        lo, hi = pl.ds(0, h), pl.ds(h, h)
        for far in (True, False):
            xx, yy = (1 - x, 1 - y) if far else (x, y)

            @pl.loop(0, NZ)
            def _(k):
                for j in range(2):
                    add(mine[u].at[k, j, xx, lo], got0[u].at[k, j, xx, lo])
                    add(mine[u].at[k, yy, j, hi], got0[u].at[k, yy, j, hi])

            if far:
                send(u, 1, mine[u].at[:, :, xx, lo], got1[u].at[0], xpeer)
                send(u, 2, mine[u].at[:, yy, :, hi], got1[u].at[1], ypeer)

    def stage2(u):
        h = mine[u].shape[3] // 2
        lo, hi = pl.ds(0, h), pl.ds(h, h)
        wait(u, 1, got1[u].at[0])
        wait(u, 2, got1[u].at[1])
        for far in (True, False):
            xx, yy = (1 - x, 1 - y) if far else (x, y)

            @pl.loop(0, NZ)
            def _(k):
                add(mine[u].at[k, yy, x, lo], got1[u].at[0, k, yy])
                add(mine[u].at[k, y, xx, hi], got1[u].at[1, k, xx])

            if far:
                send(u, 3, mine[u].at[:, yy, x, lo], got2[u].at[0], ypeer)
                send(u, 4, mine[u].at[:, y, xx, hi], got2[u].at[1], xpeer)

    def stage3(u):
        h = mine[u].shape[3] // 2
        lo, hi = pl.ds(0, h), pl.ds(h, h)
        wait(u, 3, got2[u].at[0])
        wait(u, 4, got2[u].at[1])

        @pl.loop(0, NZ)
        def _(k):
            add(mine[u].at[k, y, x, lo], got2[u].at[0, k])
            add(mine[u].at[k, y, x, hi], got2[u].at[1, k])

        for d in range(1, NZ):
            send(u, 4 + d, mine[u].at[zof[d], y, x], got3[u].at[d - 1], zpeers[d])

    def stage4(u):
        w, col, width = UNITS[u]
        for d in range(1, NZ):
            wait(u, 4 + d, got3[u].at[d - 1])
        total = mine[u][z, y, x].astype(jnp.float32)
        for d in range(1, NZ):
            total = total + got3[u][d - 1].astype(jnp.float32)
        res[u][...] = total
        cp = pltpu.make_async_copy(res[u], outs[w].at[:, pl.ds(col, width)], osem.at[u])
        cp.start()
        finals.append(cp)

    finals = []
    gain_copies = []
    for j, (peer, o) in enumerate(zip(peers, peers)):
        block = (o[0] * 4 + o[1]) // 4
        cp = remote(gain_in.at[block], got_gain.at[j + 1], gs.at[j], gr.at[j], peer)
        cp.start()
        gain_copies.append(cp)
    for t in range(nu + 4):
        for step, lag in ((stage4, 4), (stage3, 3), (stage2, 2), (stage1, 1), (stage0, 0)):
            if 0 <= t - lag < nu:
                step(t - lag)
    for cp in gain_copies:
        cp.wait()
    got_gain[0] = gain_in[owner(z, y, x, c) // 4]
    total = got_gain[0]
    for j in range(1, 32):
        total = total + got_gain[j]
    gain_out[...] = total
    for cp in pend:
        cp.wait_send()
    for cp in finals:
        cp.wait()


def scatter(grads, gains):
    hbm = pl.BlockSpec(memory_space=pl.ANY)
    vmem = pl.BlockSpec(memory_space=pltpu.VMEM)
    dims = [(g.shape[4], g.shape[5]) for g in grads]
    scratch = []
    per = [(dims[w][0], width) for w, col, width in UNITS]
    for r, n in per:
        scratch.append(pltpu.VMEM((4, 2, 2, r, n), jnp.bfloat16))
    for r, n in per:
        scratch.append(pltpu.VMEM((4, 2, 2, r, n), jnp.bfloat16))
    for r, n in per:
        scratch.append(pltpu.VMEM((2, 4, 2, r // 2, n), jnp.bfloat16))
    for r, n in per:
        scratch.append(pltpu.VMEM((2, 4, r // 2, n), jnp.bfloat16))
    for r, n in per:
        scratch.append(pltpu.VMEM((3, r, n), jnp.bfloat16))
    for r, n in per:
        scratch.append(pltpu.VMEM((r, n), jnp.float32))
    nu = len(UNITS)
    scratch += [
        pltpu.VMEM((32, 8, 128), jnp.float32),
        pltpu.SemaphoreType.DMA((nu, 8)),
        pltpu.SemaphoreType.DMA((nu, 8)),
        pltpu.SemaphoreType.DMA((nu,)),
        pltpu.SemaphoreType.DMA((nu,)),
        pltpu.SemaphoreType.DMA((31,)),
        pltpu.SemaphoreType.DMA((31,)),
    ]
    return pl.pallas_call(
        functools.partial(scatter_kernel, dims),
        out_shape=[jax.ShapeDtypeStruct(d, jnp.float32) for d in dims]
        + [jax.ShapeDtypeStruct((8, 128), jnp.float32)],
        in_specs=[hbm] * 4 + [vmem],
        out_specs=[hbm] * 4 + [vmem],
        scratch_shapes=scratch,
        compiler_params=pltpu.CompilerParams(
            collective_id=1, has_side_effects=True, vmem_limit_bytes=60 << 20
        ),
    )(*grads, gains)


def project_input(inputs, w_qkv, gain):
    normed, scale_one = normalize(inputs, gain)
    normed_low = normed.astype(jnp.bfloat16)
    mixed = jnp.dot(normed_low, w_qkv, preferred_element_type=jnp.float32).astype(jnp.bfloat16)
    split = mixed.reshape(inputs.shape[0], 3, H, HD)
    return (normed_low, scale_one, split[:, 0], split[:, 1], split[:, 2])


def feed_inputs(inputs, context, w_out, w_up, gain):
    middle = inputs + jnp.dot(context, w_out, preferred_element_type=jnp.float32)
    second, scale_two = normalize(middle, gain)
    second_low = second.astype(jnp.bfloat16)
    hidden = jnp.dot(second_low, w_up, preferred_element_type=jnp.float32)
    active = jax.nn.gelu(hidden, approximate=True).astype(jnp.bfloat16)
    return (middle, scale_two, second_low, hidden, active)


def layer(tokens, lengths, w_qkv, w_out, w_up, w_down, gain_attn, gain_mlp, cotangent, low_type):
    total_rows = tokens.shape[0]
    ends = jnp.cumsum(lengths[0])
    places = jnp.arange(total_rows, dtype=jnp.int32)
    segment = jnp.sum((places[:, None] >= ends[None, :]).astype(jnp.int32), axis=1)
    inputs = tokens.astype(jnp.float32)
    gain_attn, gain_mlp = gain_attn.astype(jnp.float32), gain_mlp.astype(jnp.float32)
    normed_low, scale_one, queries, keys_all, values_all = project_input(inputs, w_qkv, gain_attn)
    context_full, log_sums = attend_forward(queries, keys_all, values_all, segment)
    context = context_full.reshape(total_rows, H * HD).astype(jnp.bfloat16)
    middle, scale_two, second_low, hidden, active = feed_inputs(
        inputs, context, w_out, w_up, gain_mlp
    )
    output = (middle + jnp.dot(active, w_down, preferred_element_type=jnp.float32)).astype(
        jnp.bfloat16
    )
    grad_down = jnp.einsum("rf,rd->fd", active, cotangent, preferred_element_type=low_type)
    grad_active = jnp.einsum("rd,fd->rf", cotangent, w_down, preferred_element_type=jnp.float32)
    unused, gelu_pull = jax.vjp(lambda values: jax.nn.gelu(values, approximate=True), hidden)
    grad_hidden = gelu_pull(grad_active)[0].astype(jnp.bfloat16)
    grad_up = jnp.einsum("rd,rf->df", second_low, grad_hidden, preferred_element_type=low_type)
    grad_second = jnp.einsum("rf,df->rd", grad_hidden, w_up, preferred_element_type=jnp.float32)
    grad_mid_norm, grad_gain_m = norm_back(grad_second, middle, scale_two, gain_mlp)
    grad_middle = cotangent.astype(jnp.float32) + grad_mid_norm
    grad_mid_low = grad_middle.astype(jnp.bfloat16)
    grad_out = jnp.einsum("rc,rd->cd", context, grad_mid_low, preferred_element_type=low_type)
    grad_context = jnp.einsum("rd,cd->rc", grad_mid_low, w_out, preferred_element_type=jnp.float32)
    grad_context = grad_context.astype(jnp.bfloat16).reshape(total_rows, H, HD)
    grad_queries, grad_keys, grad_values = attend_backward(
        queries, keys_all, values_all, segment, log_sums, grad_context
    )
    grad_mixed = (
        jnp.stack([grad_queries, grad_keys, grad_values], axis=1)
        .reshape(total_rows, 3 * H * HD)
        .astype(jnp.bfloat16)
    )
    grad_qkv = jnp.einsum("rd,re->de", normed_low, grad_mixed, preferred_element_type=low_type)
    grad_normed = jnp.einsum("re,de->rd", grad_mixed, w_qkv, preferred_element_type=jnp.float32)
    grad_in_norm, grad_gain_a = norm_back(grad_normed, inputs, scale_one, gain_attn)
    grad_tokens = (grad_middle + grad_in_norm).astype(jnp.bfloat16)
    return (output, grad_tokens, grad_qkv, grad_out, grad_up, grad_down, grad_gain_a, grad_gain_m)


def shards_any(tokens, lengths, w_qkv, w_out, w_up, w_down, gain_attn, gain_mlp, cotangent):
    whole = gather_any(w_qkv, w_out, w_up, w_down, gain_attn, gain_mlp)
    out = layer(tokens, lengths, *whole, cotangent, jnp.float32)
    return out[:2] + sum_any(*out[2:])


def shards(tokens, lengths, w_qkv, w_out, w_up, w_down, gain_attn, gain_mlp, cotangent):
    me = lax.axis_index("dp") * 4 + lax.axis_index("fsdp")
    lanes = lax.rem(me, 4) * 32
    pair = jnp.stack([gain_attn, gain_mlp]).astype(jnp.float32)
    spot = lax.dynamic_update_slice(jnp.zeros((8, 128), jnp.float32), pair, (0, lanes))
    (f_qkv, f_out, f_up, f_down), gains = gather((w_qkv, w_out, w_up, w_down), spot)
    z, y, x, c = coords()
    order = jnp.stack([me] + [o[0] * 4 + o[1] for o in all_peers_from(z, y, x, c)])
    whole = jnp.zeros((32, 8, 128), jnp.float32).at[order].set(gains)
    whole = whole.reshape(8, 4, 8, 128).sum(axis=1)
    f_ga, f_gm = whole[:, 0].reshape(1024), whole[:, 1].reshape(1024)
    out = layer(tokens, lengths, f_qkv, f_out, f_up, f_down, f_ga, f_gm, cotangent, jnp.bfloat16)
    grad_gain = jnp.stack([out[6].reshape(8, 128), out[7].reshape(8, 128)], axis=1)
    grad_gain = jnp.pad(grad_gain, ((0, 0), (0, 6), (0, 0)))
    split = lambda g: g.reshape(4, 2, 2, 2, g.shape[0] // 32, g.shape[1])
    g_down, g_up, g_out, g_qkv, g_gain = scatter(
        (split(out[5]), split(out[4]), split(out[3]), split(out[2])), grad_gain
    )
    own = lax.dynamic_slice(g_gain, (0, lanes), (2, 32))
    return (out[0], out[1], g_qkv, g_out, g_up, g_down, own[0], own[1])


def all_peers_from(z, y, x, c):
    peers = []
    for d in range(NZ):
        for m in range(2):
            for l in range(2):
                for s in range(2):
                    if d + m + l + s:
                        peers.append(
                            device(
                                lax.rem(z + NZ - d, NZ),
                                1 - y if m else y,
                                1 - x if l else x,
                                1 - c if s else c,
                            )
                        )
    return peers


def solution(mesh):
    rows, flat = P(AXES, None), P(AXES)
    known = dict(mesh.shape) == {"dp": 8, "fsdp": 4}
    return jax.shard_map(
        shards if known else shards_any,
        mesh=mesh,
        in_specs=(rows, rows, rows, rows, rows, rows, flat, flat, rows),
        out_specs=(rows, rows, rows, rows, rows, rows, flat, flat),
        check_vma=False,
    )
```

time: 1010 us -> 460 us (0.46)
  waiting for transfers between devices: 705 us -> 0 us
  Pallas kernels: 0 us -> 271 us
  blocking collectives: 82.4 us -> 0 us
  matrix products: 156 us -> 133 us
  between operations: 14.8 us -> 1.51 us
    reduce_scatter x4 -> x0, waiting for transfers between devices: 513 us -> none  [the longest x1 187 us: sum_gradients(): lax.psum_scatter(grad_up, ('dp', 'fsdp'), scatter_dimension=0, tiled=True)]
    pallas_call x0 -> x2, Pallas kernels: none -> 271 us  [the longest x1 148 us: scatter(): pl.pallas_call(functools.partial(scatter_kernel, dims), out_shape=[jax.Sh...]
    all_gather x4 -> x0, waiting for transfers between devices: 190 us -> none  [the longest x1 74.4 us: gather_forward(): lax.all_gather(w_down, ('dp', 'fsdp'), axis=0, tiled=True)]
    unnamed x2 -> x0, blocking collectives: 82.4 us -> none
    dot_general x12, matrix products: 110 us -> 93.8 us  [the longest x1 16.7 us: feed_inputs(): hidden = jnp.dot(second_low, w_up, preferred_element_type=jnp.float32)]
  transfers between devices with their start and end apart: 8 -> 0, of which waited for: 7 -> 0; matrix products, arithmetic and copies ran while one was open for 17% -> 0% of each run, Pallas kernels for 0% -> 0%
where the time goes in v1:
time: 460 us; the launch traced here: 452 us
  Pallas kernels  271 us (59%)
  matrix products  133 us (29%)
  other arithmetic  26.3 us (6%)
  local copies, waits for them, and re-layouts  20.6 us (4%)
    pallas_call x1, Pallas kernels, scatter(): pl.pallas_call(functools.partial(scatter_kernel, dims), out_shape=[jax.Sh...  148 us
    pallas_call x1, Pallas kernels, gather(): pl.pallas_call(functools.partial(gather_body, nw), out_shape=[jax.ShapeDt...  123 us
    dot_general x1, matrix products, feed_inputs(): hidden = jnp.dot(second_low, w_up, preferred_element_type=jnp.float32)  16.7 us
    dot_general x1, matrix products, layer(): jnp.dot(active, w_down, preferred_element_type=jnp.float32)  13.4 us
    dot_general x1, matrix products, layer(): jnp.einsum('rf,rd->fd', active, cotangent, preferred_element_type=low_type)  13 us
    convert_element_type x1, other arithmetic, attend_backward(): (1.0 / math.sqrt(HD) * attn_prob * (grad_prob - inner)).astype(jnp.bfloat16)  12 us
    dot_general x1, matrix products, attend_backward(): jnp.einsum('qhd,khd->hqk', grad_context, values_all, preferred_element_ty...  10.8 us
    dot_general x1, matrix products, layer(): jnp.einsum('rd,fd->rf', cotangent, w_down, preferred_element_type=jnp.flo...  10.7 us

profile of v1, /device:TPU:0, one launch (start us, length us, event | category | flops | bytes accessed | tf_op | source)
XLA Modules:
  0.0 451.9 jit_solution(10197233180546015528)
XLA Ops:
  0.6 0.7 maximum_convert_fusion.1
  1.3 0.3 dynamic_update_slice.3.refs_4_
  1.7 0.6 copy-done.13
  2.2 122.9 %shard_map.152 = (bf16[1024,3072]{1,0:T(8,128)(2,1)}, bf16[1024,1024]{1,0:T(8,128)(2,1)}, bf16[1024,4096]{1,0:T(8,128)(2,1)}, bf16[4096,1024]{1,0:T(8,128)(2,1)}, f32[32,8,128]{2,1,0:T(8,128)}) custom-call(bf16[32,3072]{1,0:T(8,128)(2,1)} %refs_0_.1, bf16[32,1024]{1,0:T(8,128)(2,1)} %refs_1_.1, bf16[32,4096]{1,0:T(8,128)(2,1)} %refs_2_.1, ...), custom_call_target="tpu_custom_call" | custom-call | tf_op jit(solution)/shard_map/pallas_call | solution.py:239
  125.3 0.1 stack.155
  125.4 2.6 scatter_fusion
  128.0 1.5 fusion.16
  129.6 8.3 %convolution_convert_fusion = bf16[512,3072]{1,0:T(8,128)(2,1)} fusion(bf16[1024,3072]{1,0:T(8,128)(2,1)} %get-tuple-element.19, bf16[512,1024]{1,0:T(8,128)(2,1)} %param.9, f32[1024]{0:T(1024)S(1)} %bitcast.152, f32[512]{0:T(512)S(1)} %get-tuple-element.37), kind=kOutput, calls=%fused_computation.34 | convolution fusion | flops 3224895488 | bytes 10491904 | tf_op jit(solution)/shard_map/dot_general | solution.py:430
  137.8 3.2 copy.38
  141.0 0.2 reduce-window.8
  141.2 0.1 convert_reduce_fusion
  141.3 0.2 fusion.32
  141.5 7.2 %fusion.43 = (f32[16,512]{1,0:T(8,128)S(1)}, f32[16,512,512]{1,2,0:T(8,128)}) fusion(bf16[512,3,16,64]{0,3,2,1:T(8,128)(2,1)S(1)} %bitcast.134, pred[512,512]{0,1:T(8,128)(4,1)S(1)} %fusion.32), kind=kOutput, calls=%fused_computation.89 | convolution fusion | flops 549445632 | bytes 19169280 | tf_op jit(solution)/shard_map/qhd,khd->hqk/dot_general | solution.py:38
  148.8 8.3 %fusion = f32[16,512]{1,0:T(8,128)S(1)} fusion(f32[16,512,512]{1,2,0:T(8,128)} %get-tuple-element.43, f32[16,512]{1,0:T(8,128)S(1)} %get-tuple-element.42), kind=kLoop, calls=%fused_computation.7 | loop fusion | flops 8380416 | bytes 16842752 | tf_op jit(solution)/shard_map/reduce_sum | solution.py:49
  157.1 8.2 %fusion.29 = bf16[16,64,512]{2,1,0:T(8,128)(2,1)S(1)} fusion(f32[16,512,512]{1,2,0:T(8,128)} %get-tuple-element.43, f32[16,512]{1,0:T(8,128)S(1)} %fusion, f32[16,512]{1,0:T(8,128)S(1)} %get-tuple-element.42, bf16[512,3,16,64]{0,3,2,1:T(8,128)(2,1)S(1)} %bitcast.135), kind=kOutput, calls=%fused_computation.54 | convolution fusion | flops 549978112 | bytes 18939904 | tf_op jit(solution)/shard_map/hqk,khd->qhd/dot_general | solution.py:51
  165.3 1.4 multiply_reduce_fusion.3
  166.7 0.2 copy-done.9
  166.9 10.7 %fusion.44 = f32[4096,512]{0,1:T(8,128)} fusion(bf16[4096,1024]{1,0:T(8,128)(2,1)} %get-tuple-element.22, bf16[512,1024]{1,0:T(8,128)(2,1)S(1)} %copy-done.9), kind=kOutput, calls=%fused_computation.90 | convolution fusion | flops 4294967296 | bytes 17825792 | tf_op jit(solution)/shard_map/rd,fd->rf/dot_general | solution.py:461
  177.6 16.7 %fusion.8 = (bf16[512,4096]{1,0:T(8,128)(2,1)S(1)}, f32[512,4096]{1,0:T(8,128)}) fusion(f32[4096,512]{0,1:T(8,128)} %fusion.44, bf16[1024,4096]{1,0:T(8,128)(2,1)} %get-tuple-element.21, f32[512,1024]{1,0:T(8,128)S(1)} %get-tuple-element.45, f32[1024]{0:T(1024)S(1)} %bitcast.148, f32[512]{0:T(512)S(1)} %get-tuple-element.39), kind=kOutput, calls=%fused_computation.17 | convolution fusion | flops 4338483200 | bytes 31463424 | tf_op jit(solution)/shard_map/dot_general | solution.py:439
  194.3 13.4 %add_convert_fusion = bf16[512,1024]{1,0:T(8,128)(2,1)} fusion(f32[512,1024]{1,0:T(8,128)S(1)} %get-tuple-element.45, bf16[4096,1024]{1,0:T(8,128)(2,1)} %get-tuple-element.22, f32[512,4096]{1,0:T(8,128)} %get-tuple-element.47), kind=kOutput, calls=%fused_computation.48 | convolution fusion | flops 4314890240 | bytes 19922944 | tf_op jit(solution)/shard_map/dot_general | solution.py:457
  207.8 7.3 %multiply_reduce_fusion.1 = (f32[1024]{0:T(1024)S(1)}, f32[512]{0:T(512)S(1)}, f32[512,1024]{1,0:T(8,128)S(1)}) fusion(f32[512,1024]{1,0:T(8,128)S(1)} %get-tuple-element.45, f32[512]{0:T(512)S(1)} %get-tuple-element.39, f32[1024]{0:T(1024)S(1)} %bitcast.149, bf16[512,4096]{1,0:T(8,128)(2,1)S(1)} %get-tuple-element.46, bf16[1024,4096]{1,0:T(8,128)(2,1)} %get-tuple-element.21), kind=kOutput, calls=%fused_computation.45 | convolution fusion | flops 4298111488 | bytes 16789504 | tf_op jit(solution)/shard_map/rf,df->rd/dot_general | solution.py:465
  215.1 0.6 subtract_add_fusion
  215.7 1.3 copy-done.3
  217.0 2.3 convolution_convert_fusion.1
  219.2 2.3 copy.41
  221.5 8.9 %fusion.26 = bf16[512,1,16,64]{0,3,2,1:T(8,128)(2,1)S(1)} fusion(bf16[512,16,64]{0,2,1:T(8,128)(2,1)} %bitcast.139, f32[16,512,512]{1,2,0:T(8,128)} %get-tuple-element.43, f32[16,512]{1,0:T(8,128)S(1)} %log_add_fusion), kind=kOutput, calls=%fused_computation.51 | convolution fusion | flops 545259520 | bytes 18907136 | tf_op jit(solution)/shard_map/hqk,qhd->khd/dot_general | solution.py:69
  230.4 10.8 %multiply_reduce_fusion = (f32[16,512]{1,0:T(8,128)S(1)}, f32[16,512,512]{1,2,0:T(8,128)}) fusion(f32[16,512,512]{1,2,0:T(8,128)} %get-tuple-element.43, f32[16,512]{1,0:T(8,128)S(1)} %log_add_fusion, bf16[512,16,64]{0,2,1:T(8,128)(2,1)S(1)} %bitcast.140, bf16[512,3,16,64]{0,3,2,1:T(8,128)(2,1)S(1)} %bitcast.136), kind=kOutput, calls=%fused_computation.2 | convolution fusion | flops 549445632 | bytes 35717120 | tf_op jit(solution)/shard_map/qhd,khd->hqk/dot_general | solution.py:60
  241.2 12.0 %multiply_convert_fusion = bf16[16,512,512]{1,2,0:T(8,128)(2,1)S(1)} fusion(f32[16,512,512]{1,2,0:T(8,128)} %get-tuple-element.50, f32[16,512,512]{1,2,0:T(8,128)} %get-tuple-element.43, f32[16,512]{1,0:T(8,128)S(1)} %get-tuple-element.49, f32[16,512]{1,0:T(8,128)S(1)} %log_add_fusion), kind=kLoop, calls=%fused_computation.1 | loop fusion | flops 20971520 | bytes 42008576 | tf_op jit(solution)/shard_map/convert_element_type | solution.py:64
  253.2 2.6 convolution_bitcast_fusion
  255.9 1.5 convolution_bitcast_fusion.1
  257.4 0.3 maximum_convert_fusion
  257.7 0.3 slice-done.1
  258.1 0.7 copy-done.2
  258.8 3.9 fusion.25
  262.7 1.8 fusion.36
  264.5 13.0 %fusion.41 = bf16[4096,1024]{1,0:T(8,128)(2,1)} fusion(bf16[512,1024]{1,0:T(8,128)(2,1)S(1)} %copy-done.10, f32[512,4096]{1,0:T(8,128)} %get-tuple-element.47), kind=kOutput, calls=%fused_computation.87 | convolution fusion | flops 4313841664 | bytes 17825792 | tf_op jit(solution)/shard_map/rf,rd->fd/dot_general | solution.py:460
  277.5 7.0 %fusion.39 = bf16[1024,4096]{1,0:T(8,128)(2,1)} fusion(bf16[512,4096]{1,0:T(8,128)(2,1)S(1)} %copy-done.16, f32[512,1024]{1,0:T(8,128)S(1)} %copy-done.6, f32[1024]{0:T(1024)S(1)} %bitcast.151, f32[512]{0:T(512)S(1)} %get-tuple-element.39), kind=kOutput, calls=%fused_computation.85 | convolution fusion | flops 4296540160 | bytes 14686208 | tf_op jit(solution)/shard_map/rd,rf->df/dot_general | solution.py:464
  284.5 2.6 fusion.30.refs_2_
  287.1 0.5 copy.45
  287.6 7.3 %fusion.45.refs_3_ = bf16[4,2,2,2,32,3072]{5,4,3,2,1,0:T(8,128)(2,1)} fusion(bf16[4,2,2,2,32,512]{5,4,3,2,1,0:T(8,128)(2,1)S(1)} %bitcast.145, bf16[512,3072,1,1,1,1]{0,1,5,4,3,2:T(8,128)(2,1)} %bitcast.144), kind=kOutput, calls=%fused_computation.91 | convolution fusion | flops 3221225472 | bytes 10485760 | tf_op jit(solution)/shard_map/rd,re->de/dot_general | solution.py:480
  294.9 0.6 select_maximum_fusion.refs_4_
  295.5 147.6 %shard_map.153 = (f32[128,1024]{1,0:T(8,128)}, f32[32,4096]{1,0:T(8,128)}, f32[32,1024]{1,0:T(8,128)}, f32[32,3072]{1,0:T(8,128)}, f32[8,128]{1,0:T(8,128)}) custom-call(bf16[4,2,2,2,128,1024]{5,4,3,2,1,0:T(8,128)(2,1)} %bitcast.141, bf16[4,2,2,2,32,4096]{5,4,3,2,1,0:T(8,128)(2,1)} %bitcast.142, bf16[4,2,2,2,32,1024]{5,4,3,2,1,0:T(8,128)(2,1)} %fusion.30.refs_2_, ...), custom_call_target="tpu_custom_call" | custom-call | tf_op jit(solution)/shard_map/pallas_call | solution.py:414
  443.1 0.8 constant_dynamic-slice_fusion
  443.9 0.5 slice_bitcast_fusion.9
  444.4 1.8 copy.61
  446.2 1.6 copy.62
  447.8 1.9 copy.63
  449.6 1.9 copy.64
  (44 shorter events, 0.2 us)
Async XLA Ops:
  1.6 0.6 copy-start.13
  137.8 3.2 copy-start.14
  157.0 8.3 %copy-start.1 = (bf16[512,1024]{1,0:T(8,128)(2,1)S(1)}, bf16[512,1024]{1,0:T(8,128)(2,1)}, u32[]{:S(2)}) copy-start(bf16[512,1024]{1,0:T(8,128)(2,1)} %param.9) | copy-start | bytes 3145732
  157.0 8.3 %copy-start.8 = (bf16[1024,1024]{1,0:T(8,128)(2,1)S(1)}, bf16[1024,1024]{1,0:T(8,128)(2,1)}, u32[]{:S(2)}) copy-start(bf16[1024,1024]{1,0:T(8,128)(2,1)} %get-tuple-element.20) | copy-start | bytes 6291460
  165.3 12.3 %copy-start.11 = (bf16[16,64,512]{2,1,0:T(8,128)(2,1)}, bf16[16,64,512]{2,1,0:T(8,128)(2,1)S(1)}, u32[]{:S(2)}) copy-start(bf16[16,64,512]{2,1,0:T(8,128)(2,1)S(1)} %fusion.29) | copy-start | bytes 3145732
  165.3 1.6 copy-start.9
  166.7 48.4 %copy-start.5 = (f32[512,1024]{1,0:T(8,128)}, f32[512,1024]{1,0:T(8,128)S(1)}, u32[]{:S(2)}) copy-start(f32[512,1024]{1,0:T(8,128)S(1)} %get-tuple-element.45) | copy-start | bytes 6291460
  194.3 13.4 %copy-start.15 = (bf16[512,4096]{1,0:T(8,128)(2,1)}, bf16[512,4096]{1,0:T(8,128)(2,1)S(1)}, u32[]{:S(2)}) copy-start(bf16[512,4096]{1,0:T(8,128)(2,1)S(1)} %get-tuple-element.46) | copy-start | bytes 12582916
  215.7 1.3 copy-start.3
  221.5 8.9 %copy-start = (bf16[512,1024]{0,1:T(8,128)(2,1)S(1)}, bf16[512,1024]{0,1:T(8,128)(2,1)}, u32[]{:S(2)}) copy-start(bf16[512,1024]{0,1:T(8,128)(2,1)} %copy.41) | copy-start | bytes 3145732
  253.2 4.5 slice-start
  255.9 2.2 slice-start.1
  257.4 1.4 copy-start.2
  257.7 5.0 %copy-start.7 = (bf16[512,3,16,64]{0,3,2,1:T(8,128)(2,1)}, bf16[512,3,16,64]{0,3,2,1:T(8,128)(2,1)S(1)}, u32[]{:S(2)}) copy-start(bf16[512,3,16,64]{0,3,2,1:T(8,128)(2,1)S(1)} %maximum_convert_fusion) | copy-start | bytes 9437188
  258.8 4.0 copy-start.4
  262.7 1.8 copy-start.10
  264.5 13.0 %copy-start.6 = (f32[512,1024]{1,0:T(8,128)S(1)}, f32[512,1024]{1,0:T(8,128)}, u32[]{:S(2)}) copy-start(f32[512,1024]{1,0:T(8,128)} %copy-done.5) | copy-start | bytes 6291460
  264.5 13.0 %copy-start.16 = (bf16[512,4096]{1,0:T(8,128)(2,1)S(1)}, bf16[512,4096]{1,0:T(8,128)(2,1)}, u32[]{:S(2)}) copy-start(bf16[512,4096]{1,0:T(8,128)(2,1)} %copy-done.15) | copy-start | bytes 12582916
  277.5 7.0 %copy-start.12 = (bf16[16,64,512]{2,1,0:T(8,128)(2,1)S(1)}, bf16[16,64,512]{2,1,0:T(8,128)(2,1)}, u32[]{:S(2)}) copy-start(bf16[16,64,512]{2,1,0:T(8,128)(2,1)} %copy-done.11) | copy-start | bytes 3145732
